TPU v7x, 512 devices: a whole 4x4x16 slice. The times are simulated.
512 devices in a mesh: mem: 16 (over y_lo, x, core), sp: 32 (over y_hi, z).
Axes of the slice: x: 4, y: 4 (y_hi: 2, y_lo: 2; y = y_hi * 2 + y_lo), z: 16, core: 2. Of those that a mesh axis runs over, the one named last changes fastest.
Arguments:
- cycle_start_state: float32 [128, 3, 6, 24576], P('mem', None, None, 'sp'), may hold values from -6 to 6
- diffusivity: float32 [6], replicated, may hold values from 0.04 to 0.22
- coupling: float32 [3, 3], replicated, may hold values from -0.3 to 0.3
- observation_value: float32 [32, 16, 512], P('sp', 'mem'), may hold values from -8 to 8
- observation_cell: int32 [32, 16, 512], P('sp', 'mem'), may hold values from 0 to 863
- observation_lists: int32 [32, 16, 8, 256], P('sp', 'mem'), may hold values from 0 to 511
- localization_weight: float32 [32, 16, 8, 256], P('sp', 'mem'), may hold values from 0.2 to 2
Outputs:
- analysis: float32 [128, 3, 6, 24576], P('mem', None, None, 'sp')
Inputs may be any that keep to these rules, and one draw needn't show every extreme that they name: `observation_cell`: index into one member's 864 values of tile (a, b), ordered field, level, row, column. `observation_lists`: index into the 512 observations of the same tile; repeats possible.
All inputs are finite; a program needn't handle non-finite values.
Results may differ from a plain program's by a relative error of at most 0.0003.
Values sent between devices are 32-bit elements; how exact they have to be, the bound alone decides.
A program may use at most 64 MiB of HBM per device.

v0:
```python
import functools

import jax
import jax.numpy as jnp
from jax import lax
from jax.experimental import pallas as pl
from jax.experimental.pallas import tpu as pltpu
from jax.sharding import PartitionSpec as P

GX = 4
GY = 2
COARSE = 8
PIVOTS = 8
F32 = jnp.float32
BF16 = jnp.bfloat16
NT = (((1,), (1,)), ((), ()))
NN = (((1,), (0,)), ((), ()))
MESH = pl.DeviceIdType.MESH
LANES = 128
TILE_COLS = 12
HALF = 96


def lane_ids(shape):
    return lax.broadcasted_iota(jnp.int32, shape, len(shape) - 1)


def turn(x, shift):
    return pltpu.roll(x, shift % LANES, x.ndim - 1)


def swap_blocks(rows):
    rows = list(rows)
    lane = lane_ids(rows[0].shape)
    for step in (4, 2, 1):
        width = TILE_COLS * step
        keep = lane % (2 * width) < width
        for a in range(8):
            if a & step:
                continue
            low, high = rows[a], rows[a + step]
            rows[a] = jnp.where(keep, low, turn(high, width))
            rows[a + step] = jnp.where(keep, turn(low, -width), high)
    return rows


def pack_four(parts):
    lane = lane_ids(parts[0].shape)
    one, two, three = turn(parts[1], 96), turn(parts[2], 64), turn(parts[3], 32)
    return [
        jnp.where(lane < 96, parts[0], one),
        jnp.where(lane < 64, one, two),
        jnp.where(lane < 32, two, three),
    ]


def unpack_four(vecs):
    lane = lane_ids(vecs[0].shape)
    return [
        vecs[0],
        turn(jnp.where(lane < 64, vecs[1], vecs[0]), -96),
        turn(jnp.where(lane < 64, vecs[2], vecs[1]), -64),
        turn(vecs[2], -32),
    ]


def row_halves(vecs):
    lane = lane_ids(vecs[0].shape)
    first, middle, last = vecs
    return [
        (first, jnp.where(lane < 64, middle, first)),
        (turn(jnp.where(lane < 64, last, middle), 64), turn(last, 64)),
    ]


def time_step(rows, diffusion, mix):
    fields, count = len(rows), len(rows[0])
    lane = lane_ids(rows[0][0][0].shape)
    out = [[None] * (count - 2) for _ in range(fields)]
    for r in range(1, count - 1):
        pair = [[None, None] for _ in range(fields)]
        for h in range(2):
            for f in range(fields):
                center = rows[f][r][h]
                before, after = turn(center, 1), turn(center, -1)
                if h == 0:
                    before = jnp.where(lane == 0, 0.0, before)
                else:
                    after = jnp.where(lane == 63, 0.0, after)
                around = (rows[f][r - 1][h] + rows[f][r + 1][h]) + (before + after)
                new = diffusion * around
                for g in range(fields):
                    new = new + mix[f][g] * rows[g][r][h]
                pair[f][h] = new
        for f in range(fields):
            out[f][r - 1] = tuple(pair[f])
    return out


def greet(axis_sizes, partners):
    barrier = pltpu.get_barrier_semaphore()
    mem, sp = lax.axis_index("mem"), lax.axis_index("sp")
    tiles, bands = axis_sizes

    @pl.loop(1, tiles)
    def _(j):
        pl.semaphore_signal(barrier, inc=1, device_id={"mem": lax.rem(mem + j, tiles)}, device_id_type=MESH)

    if partners:

        @pl.when(sp > 0)
        def _():
            pl.semaphore_signal(barrier, inc=1, device_id={"sp": sp - 1}, device_id_type=MESH)

        @pl.when(sp < bands - 1)
        def _():
            pl.semaphore_signal(barrier, inc=1, device_id={"sp": sp + 1}, device_id_type=MESH)


def await_greetings(axis_sizes, partners):
    sp = lax.axis_index("sp")
    tiles, bands = axis_sizes
    count = tiles - 1
    if partners:
        count = count + jnp.minimum(sp, 1) + jnp.minimum(bands - 1 - sp, 1)
    pl.semaphore_wait(pltpu.get_barrier_semaphore(), count)


def forecast_kernel(
    axis_sizes, fields, levels, x_ref, diffusion_ref, coupling_ref, out_ref,
    north, south, grown, blocks, packed, landed, halo_send, halo_recv, block_send, block_recv,
):
    mem, sp = lax.axis_index("mem"), lax.axis_index("sp")
    tiles, bands = axis_sizes
    layers = fields * levels
    groups = layers // 2
    two = 3 * LANES

    greet(axis_sizes, True)
    await_greetings(axis_sizes, True)

    down = pltpu.make_async_remote_copy(
        src_ref=x_ref.at[:, :, pl.ds(two, two)], dst_ref=north, send_sem=halo_send.at[0], recv_sem=halo_recv.at[0],
        device_id={"sp": lax.rem(sp + 1, bands)}, device_id_type=MESH,
    )
    up = pltpu.make_async_remote_copy(
        src_ref=x_ref.at[:, :, pl.ds(0, two)], dst_ref=south, send_sem=halo_send.at[1], recv_sem=halo_recv.at[1],
        device_id={"sp": lax.rem(sp + bands - 1, bands)}, device_id_type=MESH,
    )

    @pl.when(sp < bands - 1)
    def _():
        down.start()

    @pl.when(sp > 0)
    def _():
        up.start()

    @pl.when(sp == 0)
    def _():
        north[...] = jnp.zeros_like(north)

    @pl.when(sp == bands - 1)
    def _():
        south[...] = jnp.zeros_like(south)

    @pl.when(sp > 0)
    def _():
        down.wait_recv()

    @pl.when(sp < bands - 1)
    def _():
        up.wait_recv()

    inside_north = jnp.minimum(sp, 1).astype(F32)
    inside_south = jnp.minimum(bands - 1 - sp, 1).astype(F32)

    @pl.loop(0, levels)
    def _(level):
        diffusion = diffusion_ref[level]
        own = 1.0 - 4.0 * diffusion
        mix = [[coupling_ref[f, g] + own if f == g else coupling_ref[f, g] for g in range(fields)] for f in range(fields)]
        rows = []
        for f in range(fields):
            layer = f * levels + level
            line = []
            for ref, starts in ((north, (0,)), (x_ref, (0, two)), (south, (0,))):
                for start in starts:
                    line += row_halves([ref[layer, :, pl.ds(start + LANES * v, LANES)] for v in range(3)])
            rows.append(line)
        middle = time_step(rows, diffusion, mix)
        for f in range(fields):
            middle[f][0] = tuple(inside_north * v for v in middle[f][0])
            middle[f][-1] = tuple(inside_south * v for v in middle[f][-1])
        final = time_step(middle, diffusion, mix)
        for f in range(fields):
            layer = f * levels + level
            for r in range(len(final[f])):
                grown[0, layer, r] = final[f][r][0]
                grown[1, layer, r] = turn(final[f][r][1], 32)

    for half in range(2):

        @pl.loop(0, groups)
        def _(group):
            rows = [grown[half, 2 * group + k // 4, k % 4] for k in range(8)]
            for b, row in enumerate(swap_blocks(rows)):
                blocks[8 * half + b, group] = row

    def fill(peer, store):
        for quad in range(groups // 4):
            for v, vec in enumerate(pack_four([blocks[peer, 4 * quad + k] for k in range(4)])):
                store(3 * quad + v, vec)
        store(3 * (groups // 4), jnp.where(lane_ids((8, LANES)) < HALF, blocks[peer, groups - 1], 0.0))

    def block_copy(peer):
        return pltpu.make_async_remote_copy(
            src_ref=packed.at[peer], dst_ref=landed.at[mem], send_sem=block_send.at[peer], recv_sem=block_recv.at[mem],
            device_id={"mem": peer}, device_id_type=MESH,
        )

    @pl.loop(1, tiles)
    def _(j):
        peer = lax.rem(mem + j, tiles)

        def store(v, vec):
            packed[peer, :, pl.ds(LANES * v, LANES)] = vec

        fill(peer, store)
        block_copy(peer).start()

    def keep(v, vec):
        landed[mem, :, pl.ds(LANES * v, LANES)] = vec

    fill(mem, keep)

    @pl.loop(1, tiles)
    def _(j):
        owner = lax.rem(mem + j, tiles)
        pltpu.make_async_remote_copy(
            src_ref=packed.at[owner], dst_ref=landed.at[owner], send_sem=block_send.at[owner],
            recv_sem=block_recv.at[owner], device_id={"mem": owner}, device_id_type=MESH,
        ).wait_recv()

    @pl.loop(0, tiles)
    def _(j):
        out_ref[j] = landed[j]

    @pl.loop(1, tiles)
    def _(j):
        block_copy(lax.rem(mem + j, tiles)).wait_send()

    @pl.when(sp < bands - 1)
    def _():
        down.wait_send()

    @pl.when(sp > 0)
    def _():
        up.wait_send()


def forecast(x, diffusivity, coupling, axis_sizes):
    fields, levels = coupling.shape[0], diffusivity.shape[0]
    layers, members, _ = x.shape
    tiles = axis_sizes[0]
    groups = layers // 2
    width = LANES * (-(-layers * 4 * TILE_COLS // LANES))
    vmem, smem = pl.BlockSpec(memory_space=pltpu.VMEM), pl.BlockSpec(memory_space=pltpu.SMEM)
    return pl.pallas_call(
        functools.partial(forecast_kernel, axis_sizes, fields, levels),
        out_shape=jax.ShapeDtypeStruct((tiles, members, width), F32),
        in_specs=[vmem, smem, smem],
        out_specs=vmem,
        scratch_shapes=[
            pltpu.VMEM((layers, members, 3 * LANES), F32),
            pltpu.VMEM((layers, members, 3 * LANES), F32),
            pltpu.VMEM((2, layers, 4, members, LANES), F32),
            pltpu.VMEM((tiles, groups, members, LANES), F32),
            pltpu.VMEM((tiles, members, width), F32),
            pltpu.VMEM((tiles, members, width), F32),
            pltpu.SemaphoreType.DMA((2,)),
            pltpu.SemaphoreType.DMA((2,)),
            pltpu.SemaphoreType.DMA((tiles,)),
            pltpu.SemaphoreType.DMA((tiles,)),
        ],
        compiler_params=pltpu.CompilerParams(
            collective_id=0, has_side_effects=True, vmem_limit_bytes=32 * 1024 * 1024
        ),
    )(x, diffusivity, coupling)


def return_kernel(axis_sizes, a_ref, out_ref, landed, blocks, send, recv):
    mem = lax.axis_index("mem")
    tiles = axis_sizes[0]
    groups = blocks.shape[1]

    greet(axis_sizes, False)
    await_greetings(axis_sizes, False)

    def block_copy(peer, slot):
        return pltpu.make_async_remote_copy(
            src_ref=a_ref.at[peer], dst_ref=landed.at[slot], send_sem=send.at[peer], recv_sem=recv.at[slot],
            device_id={"mem": peer}, device_id_type=MESH,
        )

    @pl.loop(1, tiles)
    def _(j):
        block_copy(lax.rem(mem + j, tiles), mem).start()

    landed[mem] = a_ref[mem]

    def spread_out(owner):
        for quad in range(groups // 4):
            vecs = [landed[owner, :, pl.ds(LANES * (3 * quad + v), LANES)] for v in range(3)]
            for k, part in enumerate(unpack_four(vecs)):
                blocks[owner, 4 * quad + k] = part
        blocks[owner, groups - 1] = landed[owner, :, pl.ds(LANES * 3 * (groups // 4), LANES)]

    spread_out(mem)

    @pl.loop(1, tiles)
    def _(j):
        owner = lax.rem(mem + tiles - j, tiles)
        block_copy(owner, owner).wait_recv()
        spread_out(owner)

    @pl.loop(0, groups)
    def _(group):
        halves = [swap_blocks([blocks[8 * half + b, group] for b in range(8)]) for half in range(2)]
        for pair in range(4):
            parts = [halves[k % 2][2 * pair + k // 2] for k in range(4)]
            for v, vec in enumerate(pack_four(parts)):
                out_ref[2 * group + pair // 2, :, pl.ds(LANES * (3 * (pair % 2) + v), LANES)] = vec

    @pl.loop(1, tiles)
    def _(j):
        block_copy(lax.rem(mem + j, tiles), mem).wait_send()


def give_back(blocks, layers, axis_sizes):
    tiles, members, width = blocks.shape
    vmem = pl.BlockSpec(memory_space=pltpu.VMEM)
    return pl.pallas_call(
        functools.partial(return_kernel, axis_sizes),
        out_shape=jax.ShapeDtypeStruct((layers, members, 4 * TILE_COLS * tiles), F32),
        in_specs=[vmem],
        out_specs=vmem,
        scratch_shapes=[
            pltpu.VMEM((tiles, members, width), F32),
            pltpu.VMEM((tiles, layers // 2, members, LANES), F32),
            pltpu.SemaphoreType.DMA((tiles,)),
            pltpu.SemaphoreType.DMA((tiles,)),
        ],
        compiler_params=pltpu.CompilerParams(
            collective_id=1, has_side_effects=True, vmem_limit_bytes=32 * 1024 * 1024
        ),
    )(blocks)


def dot(a, b, dims):
    return lax.dot_general(a, b, dims, preferred_element_type=F32)


def split2(x):
    hi = x.astype(BF16)
    lo = (x - hi.astype(F32)).astype(BF16)
    return hi, lo


def split3(x):
    hi = x.astype(BF16)
    rest = x - hi.astype(F32)
    mid = rest.astype(BF16)
    lo = (rest - mid.astype(F32)).astype(BF16)
    return hi, mid, lo


def observation_sums(lists, scales, observed, cells, lanes):
    nobs = observed.shape[1]
    points, nloc = lists.shape
    pieces = jnp.concatenate(split3(scales), axis=0)
    which = lax.broadcasted_iota(jnp.int32, (nobs, nloc), 0)
    row = lax.broadcasted_iota(jnp.int32, (points, nobs), 0)
    per_obs = jnp.zeros((points, nobs), F32)
    for c in range(points):
        picked = jnp.where(lists[c : c + 1, :] == which, 1.0, 0.0).astype(BF16)
        got = dot(pieces, picked, NT)
        got = got[:points] + got[points : 2 * points] + got[2 * points :]
        per_obs = jnp.where(row == c, got, per_obs)
    both = jnp.concatenate(split3(per_obs) + split3(per_obs * observed), axis=0)
    place = lax.broadcasted_iota(jnp.int32, (lanes, nobs), 0)
    spots = jnp.where(cells == place, 1.0, 0.0).astype(BF16)
    got = dot(both, spots, NT)
    p = points
    weight = got[:p] + got[p : 2 * p] + got[2 * p : 3 * p]
    total = got[3 * p : 4 * p] + got[4 * p : 5 * p] + got[5 * p :]
    return weight, total


def factor_inverses(r_ref, members):
    p = COARSE
    lane = lax.broadcasted_iota(jnp.int32, (p, members), 1)

    def spread(v, i):
        return jnp.broadcast_to(v[:, i : i + 1], v.shape)

    for k0 in range(0, members, PIVOTS):
        rows = [r_ref[pl.ds(p * (k0 + t), p), :] for t in range(PIVOTS)]
        done = []
        for t in range(PIVOTS):
            k = k0 + t
            pivot = spread(rows[t], k)
            own = jnp.where(lane == k, 1.0, rows[t])
            unit = own * (1.0 / pivot)
            for s in range(t + 1, PIVOTS):
                rows[s] = jnp.where(lane == k, 0.0, rows[s]) - spread(rows[t], k0 + s) * unit
            done.append(own * lax.rsqrt(pivot))
        for t in range(PIVOTS):
            r_ref[pl.ds(p * (k0 + t), p), :] = jnp.where(lane <= k0 + t, done[t], 0.0)
        block = (lane >= k0) & (lane < k0 + PIVOTS)
        kept = [jnp.where(block & (lane > k0 + t), 0.0, done[t]) for t in range(PIVOTS)]
        for i in range(k0 + PIVOTS, members):
            acc = jnp.where(block, 0.0, r_ref[pl.ds(p * i, p), :])
            for t in range(PIVOTS):
                acc = acc - spread(done[t], i) * kept[t]
            r_ref[pl.ds(p * i, p), :] = acc


def analysis_kernel(field_ref, lists_ref, scales_ref, observed_ref, cells_ref, hats_ref, out_ref, r_ref):
    members, lanes = field_ref.shape
    p = COARSE
    weight, total = observation_sums(lists_ref[...], scales_ref[...], observed_ref[...], cells_ref[...], lanes)
    field = field_ref[...]
    mean = jnp.sum(field, axis=0, keepdims=True) * (1.0 / members)
    dev = field - mean
    hi, lo = split2(dev)
    lead = float(members - 1)
    eye = jnp.where(
        lax.broadcasted_iota(jnp.int32, (members, members), 0) == lax.broadcasted_iota(jnp.int32, (members, members), 1),
        lead,
        0.0,
    )
    for c in range(p):
        s_hi, s_lo = split2(dev * weight[c : c + 1, :])
        g = dot(s_hi, hi, NT) + dot(s_hi, lo, NT) + dot(s_lo, hi, NT) + eye
        r_ref[pl.ds(c, members, stride=p), :] = g
    gap = total - mean * weight
    g_hi, g_lo = split2(gap)
    pull = dot(g_hi, hi, NT) + dot(g_hi, lo, NT) + dot(g_lo, hi, NT)

    factor_inverses(r_ref, members)

    root = lead**0.5
    moved = jnp.zeros((members, lanes), F32)
    for c in range(p):
        m = r_ref[pl.ds(c, members, stride=p), :]
        y = lax.dot_general(pull[c : c + 1, :], m, NT, precision=lax.Precision.HIGHEST, preferred_element_type=F32)
        w = lax.dot_general(y, m, NN, precision=lax.Precision.HIGHEST, preferred_element_type=F32)
        w_hi, w_lo = split2(m * root + w)
        moved = moved + hats_ref[c : c + 1, :] * (dot(w_hi, hi, NN) + dot(w_hi, lo, NN) + dot(w_lo, hi, NN))
    out_ref[...] = mean + moved


def analyse(field, lists, scales, observed, cells, hats):
    members, lanes = field.shape
    return pl.pallas_call(
        analysis_kernel,
        out_shape=jax.ShapeDtypeStruct((members, lanes), F32),
        in_specs=[pl.BlockSpec(memory_space=pltpu.VMEM)] * 6,
        out_specs=pl.BlockSpec(memory_space=pltpu.VMEM),
        scratch_shapes=[pltpu.VMEM((COARSE * members, members), F32)],
        compiler_params=pltpu.CompilerParams(vmem_limit_bytes=48 * 1024 * 1024),
    )(field, lists, scales, observed, cells, hats)


def hat_table(row_stack, cols):
    row_pos = jnp.arange(row_stack, dtype=jnp.float32)
    col_pos = jnp.arange(cols, dtype=jnp.float32)
    span_y = (row_stack - 1) / (GY - 1)
    span_x = (cols - 1) / (GX - 1)
    centre_y = jnp.arange(GY, dtype=jnp.float32) * span_y
    centre_x = jnp.arange(GX, dtype=jnp.float32) * span_x
    hat_y = jnp.maximum(0.0, 1.0 - jnp.abs(row_pos[None, :] - centre_y[:, None]) / span_y)
    hat_x = jnp.maximum(0.0, 1.0 - jnp.abs(col_pos[None, :] - centre_x[:, None]) / span_x)
    hats = hat_y[:, None, :, None] * hat_x[None, :, None, :]
    return hats.reshape(GY * GX, row_stack * cols)


def on_device(
    axis_sizes,
    cycle_start_state,
    diffusivity,
    coupling,
    observation_value,
    observation_cell,
    observation_lists,
    localization_weight,
):
    members, fields, levels, span = cycle_start_state.shape
    layers = fields * levels
    x = cycle_start_state.transpose(1, 2, 0, 3).reshape(layers, members, span)
    columns = forecast(x, diffusivity, coupling, axis_sizes)
    tiles, _, width = columns.shape
    hats = jnp.tile(hat_table(4, TILE_COLS), (1, layers))
    analysed = analyse(
        columns.reshape(tiles * members, width),
        observation_lists[0, 0],
        localization_weight[0, 0],
        observation_value[0],
        observation_cell[0],
        jnp.pad(hats, ((0, 0), (0, width - hats.shape[1]))),
    )
    y = give_back(analysed.reshape(tiles, members, width), layers, axis_sizes)
    return y.reshape(fields, levels, members, span).transpose(2, 0, 1, 3)


def solution(mesh):
    in_specs = (
        P("mem", None, None, "sp"),
        P(),
        P(),
        P("sp", "mem", None),
        P("sp", "mem", None),
        P("sp", "mem", None, None),
        P("sp", "mem", None, None),
    )
    out_specs = P("mem", None, None, "sp")
    axis_sizes = (mesh.shape["mem"], mesh.shape["sp"])
    return jax.shard_map(
        functools.partial(on_device, axis_sizes), mesh=mesh, in_specs=in_specs, out_specs=out_specs, check_vma=False
    )
```

profile of v0, /device:TPU:17, one launch (start us, length us, event | category | flops | bytes accessed | tf_op | source)
XLA Modules:
  0.0 78.7 jit_solution(10295943402652359869)
XLA Ops:
  0.0 0.1 subtract_maximum_fusion.1
  0.1 0.1 subtract_maximum_fusion
  0.2 0.1 broadcast_multiply_fusion
  0.2 0.1 mul.39
  0.3 0.1 tile.9
  0.4 0.0 copy-start.3
  0.4 0.0 copy-start.6
  0.5 0.6 copy-done.3
  1.1 0.0 copy-done.6
  1.1 0.0 copy-start
  1.1 1.0 %copy-done = f32[8,3,6,768]{3,0,2,1:T(8,128)S(1)} copy-done((f32[8,3,6,768]{3,0,2,1:T(8,128)S(1)}, f32[8,3,6,768]{3,0,2,1:T(8,128)}, u32[]{:S(2)}) %copy-start) | copy-done | bytes 442392
  2.1 0.0 copy-start.1
  2.1 0.0 copy-start.2
  2.1 0.0 copy-start.4
  2.1 0.0 copy-start.5
  2.1 34.2 %shard_map.73 = f32[16,8,896]{2,1,0:T(8,128)S(1)} custom-call(f32[18,8,768]{2,1,0:T(8,128)S(1)} %bitcast.15, f32[6]{0:T(128)S(1)} %copy-done.6, f32[3,3]{1,0:T(4,128)S(1)} %copy-done.3), custom_call_target="tpu_custom_call" | custom-call | tf_op jit(solution)/shard_map/pallas_call | solution.py:269
  36.4 0.0 copy-done.1
  36.4 0.0 copy-done.2
  36.4 0.0 copy-done.4
  36.4 0.0 copy-done.5
  36.4 27.4 %shard_map.74 = f32[128,896]{1,0:T(8,128)S(1)} custom-call(f32[128,896]{1,0:T(8,128)S(1)} %bitcast.13, s32[8,256]{1,0:T(8,128)S(1)} %bitcast.16, f32[8,256]{1,0:T(8,128)S(1)} %bitcast.17, f32[1,512]{1,0:T(1,128)S(1)} %bitcast.18, s32[1,512]{1,0:T(1,128)S(1)} %bitcast.19, f32[8,896]{1,0:T(8,128)S(1)} %pad.4.hats_ref), custom_call_target="tpu_custom_call" | custom-call | tf_op jit(solution)/shard_map/pallas_call | solution.py:466
  63.9 14.1 %shard_map.75 = f32[18,8,768]{2,1,0:T(8,128)S(1)} custom-call(f32[16,8,896]{2,1,0:T(8,128)S(1)} %bitcast.12), custom_call_target="tpu_custom_call" | custom-call | tf_op jit(solution)/shard_map/pallas_call | solution.py:343
  77.9 0.8 copy.9
  (4 shorter events, 0.0 us)
Async XLA Ops:
  0.4 0.7 copy-start.3
  0.4 0.7 copy-start.6
  1.1 1.0 %copy-start = (f32[8,3,6,768]{3,0,2,1:T(8,128)S(1)}, f32[8,3,6,768]{3,0,2,1:T(8,128)}, u32[]{:S(2)}) copy-start(f32[8,3,6,768]{3,0,2,1:T(8,128)} %param.7) | copy-start | bytes 1327108
  2.1 34.2 %copy-start.1 = (s32[1,1,8,256]{3,2,1,0:T(8,128)S(1)}, s32[1,1,8,256]{3,2,1,0:T(8,128)}, u32[]{:S(2)}) copy-start(s32[1,1,8,256]{3,2,1,0:T(8,128)} %param.12) | copy-start | bytes 24580
  2.1 34.2 %copy-start.2 = (f32[1,1,8,256]{3,2,1,0:T(8,128)S(1)}, f32[1,1,8,256]{3,2,1,0:T(8,128)}, u32[]{:S(2)}) copy-start(f32[1,1,8,256]{3,2,1,0:T(8,128)} %param.13) | copy-start | bytes 24580
  2.1 34.3 %copy-start.4 = (f32[1,1,512]{2,1,0:T(1,128)S(1)}, f32[1,1,512]{2,1,0:T(1,128)}, u32[]{:S(2)}) copy-start(f32[1,1,512]{2,1,0:T(1,128)} %param.10) | copy-start | bytes 6148
  2.1 34.3 %copy-start.5 = (s32[1,1,512]{2,1,0:T(1,128)S(1)}, s32[1,1,512]{2,1,0:T(1,128)}, u32[]{:S(2)}) copy-start(s32[1,1,512]{2,1,0:T(1,128)} %param.11) | copy-start | bytes 6148
where the time goes:
time: 78.9 us; the launch traced here: 78.7 us
  Pallas kernels  75.7 us (96%)
  local copies, waits for them, and re-layouts  2.64 us (3%)
    pallas_call x1, Pallas kernels, forecast(): pl.pallas_call(functools.partial(forecast_kernel, axis_sizes, fields, lev...  34.2 us
    pallas_call x1, Pallas kernels, analyse(): pl.pallas_call(analysis_kernel, out_shape=jax.ShapeDtypeStruct((members,...  27.4 us
    pallas_call x1, Pallas kernels, give_back(): pl.pallas_call(functools.partial(return_kernel, axis_sizes), out_shape=ja...  14.1 us
    unnamed x15, local copies, waits for them, and re-layouts  2.45 us

commit v1 on v0

v1 whole, which is shorter than its diff:
```python
import functools

import jax
import jax.numpy as jnp
from jax import lax
from jax.experimental import pallas as pl
from jax.experimental.pallas import tpu as pltpu
from jax.sharding import PartitionSpec as P

GX = 4
GY = 2
COARSE = 8
PIVOTS = 8
PANEL = 16
F32 = jnp.float32
BF16 = jnp.bfloat16
NT = (((1,), (1,)), ((), ()))
NN = (((1,), (0,)), ((), ()))
TN = (((0,), (0,)), ((), ()))
MESH = pl.DeviceIdType.MESH
LANES = 128
TILE_ROWS = 4
TILE_COLS = 12
HALF = 96


def dot(a, b, dims):
    return lax.dot_general(a, b, dims, preferred_element_type=F32)


def split2(x):
    hi = x.astype(BF16)
    lo = (x - hi.astype(F32)).astype(BF16)
    return hi, lo


def split3(x):
    hi = x.astype(BF16)
    rest = x - hi.astype(F32)
    mid = rest.astype(BF16)
    lo = (rest - mid.astype(F32)).astype(BF16)
    return hi, mid, lo


def observation_sums(lists, scales, observed, cells, lanes):
    nobs = observed.shape[1]
    points, nloc = lists.shape
    pieces = jnp.concatenate(split3(scales), axis=0)
    which = lax.broadcasted_iota(jnp.int32, (nobs, nloc), 0)
    row = lax.broadcasted_iota(jnp.int32, (points, nobs), 0)
    per_obs = jnp.zeros((points, nobs), F32)
    for c in range(points):
        picked = jnp.where(lists[c : c + 1, :] == which, 1.0, 0.0).astype(BF16)
        got = dot(pieces, picked, NT)
        got = got[:points] + got[points : 2 * points] + got[2 * points :]
        per_obs = jnp.where(row == c, got, per_obs)
    both = jnp.concatenate(split3(per_obs) + split3(per_obs * observed), axis=0)
    place = lax.broadcasted_iota(jnp.int32, (lanes, nobs), 0)
    spots = jnp.where(cells == place, 1.0, 0.0).astype(BF16)
    got = dot(both, spots, NT)
    p = points
    weight = got[:p] + got[p : 2 * p] + got[2 * p : 3 * p]
    total = got[3 * p : 4 * p] + got[4 * p : 5 * p] + got[5 * p :]
    return weight, total


def factor_inverses(g_ref, r_ref):
    p, members, _ = g_ref.shape
    lane = lax.broadcasted_iota(jnp.int32, (p, members), 1)
    panel_lane = lax.broadcasted_iota(jnp.int32, (PANEL, members), 1)
    panel_row = lax.broadcasted_iota(jnp.int32, (PANEL, members), 0)

    def spread(v, i):
        return jnp.broadcast_to(v[:, i : i + 1], v.shape)

    for b0 in range(0, members, PANEL):
        for c in range(p):
            r_ref[pl.ds(c, PANEL, stride=p), :] = g_ref[c, pl.ds(b0, PANEL), :]
        for k0 in range(0, PANEL, PIVOTS):
            at = b0 + k0
            rows = [r_ref[pl.ds(p * (k0 + t), p), :] for t in range(PIVOTS)]
            e = [[spread(rows[t], at + s) for t in range(s + 1)] for s in range(PIVOTS)]
            block = (lane >= at) & (lane < at + PIVOTS)
            rows = [jnp.where(block, jnp.where(lane == at + t, 1.0, 0.0), rows[t]) for t in range(PIVOTS)]
            for t in range(PIVOTS):
                inverse = 1.0 / e[t][t]
                for s in range(t + 1, PIVOTS):
                    ratio = e[s][t] * inverse
                    for j in range(t + 1, s + 1):
                        e[s][j] = e[s][j] - ratio * e[j][t]
                    rows[s] = rows[s] - ratio * rows[t]
            done = [rows[t] * lax.rsqrt(e[t][t]) for t in range(PIVOTS)]
            for t in range(PIVOTS):
                r_ref[pl.ds(p * (k0 + t), p), :] = done[t]
            for i in range(k0 + PIVOTS, PANEL):
                acc = jnp.where(block, 0.0, r_ref[pl.ds(p * i, p), :])
                for t in range(PIVOTS):
                    acc = acc - spread(done[t], b0 + i) * done[t]
                r_ref[pl.ds(p * i, p), :] = acc
        end = b0 + PANEL
        for c in range(p):
            v = r_ref[pl.ds(c, PANEL, stride=p), :]
            lower = panel_lane <= panel_row + b0
            g_ref[c, pl.ds(b0, PANEL), :] = jnp.where(lower, v, 0.0)
            if end < members:
                hi, mid, lo = split3(v)
                kept = jnp.where(lower | (panel_lane >= end), 1.0, 0.0).astype(BF16)
                k_hi, k_mid, k_lo = hi * kept, mid * kept, lo * kept
                left = jnp.concatenate([hi, hi, mid, hi, mid, lo], axis=0)
                right = jnp.concatenate([k_hi, k_mid, k_hi, k_lo, k_mid, k_hi], axis=0)
                change = dot(left[:, end:] if end % 128 == 0 else left, right, TN)
                below = g_ref[c, pl.ds(end, members - end), :]
                low_lane = lax.broadcasted_iota(jnp.int32, below.shape, 1)
                below = jnp.where((low_lane >= b0) & (low_lane < end), 0.0, below)
                g_ref[c, pl.ds(end, members - end), :] = below - change[end:, :]


def lane_ids(shape):
    return lax.broadcasted_iota(jnp.int32, shape, len(shape) - 1)


def turn(x, shift):
    return pltpu.roll(x, shift % LANES, x.ndim - 1)


def swap_blocks(rows):
    rows = list(rows)
    lane = lane_ids(rows[0].shape)
    for step in (4, 2, 1):
        width = TILE_COLS * step
        keep = lane % (2 * width) < width
        for a in range(8):
            if a & step:
                continue
            low, high = rows[a], rows[a + step]
            rows[a] = jnp.where(keep, low, turn(high, width))
            rows[a + step] = jnp.where(keep, turn(low, -width), high)
    return rows


def pack_four(parts):
    lane = lane_ids(parts[0].shape)
    one, two, three = turn(parts[1], 96), turn(parts[2], 64), turn(parts[3], 32)
    return [
        jnp.where(lane < 96, parts[0], one),
        jnp.where(lane < 64, one, two),
        jnp.where(lane < 32, two, three),
    ]


def unpack_four(vecs):
    lane = lane_ids(vecs[0].shape)
    return [
        vecs[0],
        turn(jnp.where(lane < 64, vecs[1], vecs[0]), -96),
        turn(jnp.where(lane < 64, vecs[2], vecs[1]), -64),
        turn(vecs[2], -32),
    ]


def row_halves(vecs):
    lane = lane_ids(vecs[0].shape)
    first, middle, last = vecs
    return [
        (first, jnp.where(lane < 64, middle, first)),
        (turn(jnp.where(lane < 64, last, middle), 64), turn(last, 64)),
    ]


def time_step(rows, diffusion, mix):
    fields, count = len(rows), len(rows[0])
    lane = lane_ids(rows[0][0][0].shape)
    out = [[None] * (count - 2) for _ in range(fields)]
    for r in range(1, count - 1):
        pair = [[None, None] for _ in range(fields)]
        for h in range(2):
            for f in range(fields):
                center = rows[f][r][h]
                before, after = turn(center, 1), turn(center, -1)
                if h == 0:
                    before = jnp.where(lane == 0, 0.0, before)
                else:
                    after = jnp.where(lane == 63, 0.0, after)
                around = (rows[f][r - 1][h] + rows[f][r + 1][h]) + (before + after)
                new = diffusion * around
                for g in range(fields):
                    new = new + mix[f][g] * rows[g][r][h]
                pair[f][h] = new
        for f in range(fields):
            out[f][r - 1] = tuple(pair[f])
    return out


def hat_rows(lanes):
    lane = lax.broadcasted_iota(jnp.int32, (1, lanes), 1) % (TILE_ROWS * TILE_COLS)
    row, col = (lane // TILE_COLS).astype(F32), (lane % TILE_COLS).astype(F32)
    span_y, span_x = (TILE_ROWS - 1) / (GY - 1), (TILE_COLS - 1) / (GX - 1)
    hat_y = [jnp.maximum(0.0, 1.0 - jnp.abs(row - i * span_y) / span_y) for i in range(GY)]
    hat_x = [jnp.maximum(0.0, 1.0 - jnp.abs(col - j * span_x) / span_x) for j in range(GX)]
    return [y * x for y in hat_y for x in hat_x]


def analyse(field, weight, total, g_ref, r_ref):
    members, lanes = field.shape
    p = COARSE
    mean = jnp.sum(field, axis=0, keepdims=True) * (1.0 / members)
    dev = field - mean
    hi, mid, lo = split3(dev)
    both = jnp.concatenate([hi, mid], axis=0)
    lead = float(members - 1)
    eye = jnp.where(
        lax.broadcasted_iota(jnp.int32, (members, members), 0) == lax.broadcasted_iota(jnp.int32, (members, members), 1),
        lead,
        0.0,
    )
    for c in range(p):
        s_hi, s_mid, s_lo = split3(dev * weight[c : c + 1, :])
        g = dot(s_hi, both, NT) + dot(s_mid, both, NT)
        g_ref[c] = g[:, :members] + g[:, members:] + (dot(s_hi, lo, NT) + dot(s_lo, hi, NT)) + eye
    gap = total - mean * weight
    g_hi, g_mid, g_lo = split3(gap)
    pull = dot(g_hi, both, NT) + dot(g_mid, both, NT)
    pull = pull[:, :members] + pull[:, members:] + (dot(g_hi, lo, NT) + dot(g_lo, hi, NT))

    factor_inverses(g_ref, r_ref)

    root = lead**0.5
    ms = [g_ref[c] for c in range(p)]
    high = dict(precision=lax.Precision.HIGHEST, preferred_element_type=F32)
    ys = [lax.dot_general(pull[c : c + 1, :], ms[c], NT, **high) for c in range(p)]
    ws = [lax.dot_general(ys[c], ms[c], NN, **high) for c in range(p)]
    hats = hat_rows(lanes)
    moved = mean
    for c in range(p):
        w_hi, w_lo = split2(ms[c] * root + ws[c])
        twice = jnp.concatenate([w_hi, w_hi], axis=1)
        moved = moved + hats[c] * (dot(twice, both, NN) + dot(w_lo, hi, NN))
    return moved


def peer_order(mem):
    side, place, core = mem // 8, mem // 2 % 4, mem % 2
    far_first = [(1, 2), (0, 2), (1, 1), (1, 3), (1, 0), (0, 1), (0, 3), (0, 0)]
    peers = []
    for d_side, d_place in far_first:
        for d_core in range(2):
            if d_side or d_place or d_core:
                peers.append((side + d_side) % 2 * 8 + (place + d_place) % 4 * 2 + (core + d_core) % 2)
    return peers


def cycle_kernel(
    axis_sizes, fields, levels, x_ref, diffusion_ref, coupling_ref, observed_ref, cells_ref, lists_ref, scales_ref, out_ref,
    xs, north, south, grown, blocks, packed, landed, result, returned, weight_ref, total_ref, g_ref, r_ref,
    load_sem, halo_send, halo_recv, block_send, block_recv, back_send, back_recv,
):
    mem, sp = lax.axis_index("mem"), lax.axis_index("sp")
    tiles, bands = axis_sizes
    layers = fields * levels
    groups = layers // 2
    two = 3 * LANES
    members, width = packed.shape[1:]
    peers = peer_order(mem)

    load = pltpu.make_async_copy(x_ref, xs, load_sem)
    load.start()
    barrier = pltpu.get_barrier_semaphore()

    @pl.when(sp > 0)
    def _():
        pl.semaphore_signal(barrier, inc=1, device_id={"sp": sp - 1}, device_id_type=MESH)

    @pl.when(sp < bands - 1)
    def _():
        pl.semaphore_signal(barrier, inc=1, device_id={"sp": sp + 1}, device_id_type=MESH)

    for peer in peers:
        pl.semaphore_signal(barrier, inc=1, device_id={"mem": peer}, device_id_type=MESH)
    pl.semaphore_wait(barrier, tiles - 1 + jnp.minimum(sp, 1) + jnp.minimum(bands - 1 - sp, 1))

    down = pltpu.make_async_remote_copy(
        src_ref=x_ref.at[:, :, pl.ds(two, two)], dst_ref=north, send_sem=halo_send.at[0], recv_sem=halo_recv.at[0],
        device_id={"sp": lax.rem(sp + 1, bands)}, device_id_type=MESH,
    )
    up = pltpu.make_async_remote_copy(
        src_ref=x_ref.at[:, :, pl.ds(0, two)], dst_ref=south, send_sem=halo_send.at[1], recv_sem=halo_recv.at[1],
        device_id={"sp": lax.rem(sp + bands - 1, bands)}, device_id_type=MESH,
    )

    @pl.when(sp < bands - 1)
    def _():
        down.start()

    @pl.when(sp > 0)
    def _():
        up.start()

    @pl.when(sp == 0)
    def _():
        north[...] = jnp.zeros_like(north)

    @pl.when(sp == bands - 1)
    def _():
        south[...] = jnp.zeros_like(south)

    weight, total = observation_sums(lists_ref[...], scales_ref[...], observed_ref[...], cells_ref[...], width)
    weight_ref[...] = weight
    total_ref[...] = total
    load.wait()

    @pl.when(sp > 0)
    def _():
        down.wait_recv()

    @pl.when(sp < bands - 1)
    def _():
        up.wait_recv()

    inside_north = jnp.minimum(sp, 1).astype(F32)
    inside_south = jnp.minimum(bands - 1 - sp, 1).astype(F32)

    @pl.loop(0, levels)
    def _(level):
        diffusion = diffusion_ref[level]
        own = 1.0 - 4.0 * diffusion
        mix = [[coupling_ref[f, g] + own if f == g else coupling_ref[f, g] for g in range(fields)] for f in range(fields)]
        rows = []
        for f in range(fields):
            layer = f * levels + level
            line = []
            for ref, starts in ((north, (0,)), (xs, (0, two)), (south, (0,))):
                for start in starts:
                    line += row_halves([ref[layer, :, pl.ds(start + LANES * v, LANES)] for v in range(3)])
            rows.append(line)
        middle = time_step(rows, diffusion, mix)
        for f in range(fields):
            middle[f][0] = tuple(inside_north * v for v in middle[f][0])
            middle[f][-1] = tuple(inside_south * v for v in middle[f][-1])
        final = time_step(middle, diffusion, mix)
        for f in range(fields):
            layer = f * levels + level
            for r in range(len(final[f])):
                grown[0, layer, r] = final[f][r][0]
                grown[1, layer, r] = turn(final[f][r][1], 32)

    for half in range(2):

        @pl.loop(0, groups)
        def _(group):
            rows = [grown[half, 2 * group + k // 4, k % 4] for k in range(8)]
            for b, row in enumerate(swap_blocks(rows)):
                blocks[8 * half + b, group] = row

    def fill(peer, store):
        for quad in range(groups // 4):
            for v, vec in enumerate(pack_four([blocks[peer, 4 * quad + k] for k in range(4)])):
                store(3 * quad + v, vec)
        store(3 * (groups // 4), jnp.where(lane_ids((members, LANES)) < HALF, blocks[peer, groups - 1], 0.0))

    def block_copy(peer, slot):
        return pltpu.make_async_remote_copy(
            src_ref=packed.at[peer], dst_ref=landed.at[slot], send_sem=block_send.at[peer], recv_sem=block_recv.at[slot],
            device_id={"mem": peer}, device_id_type=MESH,
        )

    for peer in peers:

        def store(v, vec):
            packed[peer, :, pl.ds(LANES * v, LANES)] = vec

        fill(peer, store)
        block_copy(peer, mem).start()

    def keep(v, vec):
        landed[mem, :, pl.ds(LANES * v, LANES)] = vec

    fill(mem, keep)
    for peer in peers[::-1]:
        block_copy(peer, peer).wait_recv()

    moved = analyse(landed[...].reshape(tiles * members, width), weight_ref[...], total_ref[...], g_ref, r_ref)
    result[...] = moved.reshape(tiles, members, width)

    def back_copy(peer, slot):
        return pltpu.make_async_remote_copy(
            src_ref=result.at[peer], dst_ref=returned.at[slot], send_sem=back_send.at[peer], recv_sem=back_recv.at[slot],
            device_id={"mem": peer}, device_id_type=MESH,
        )

    for peer in peers:
        back_copy(peer, mem).start()
    for peer in peers:
        block_copy(peer, mem).wait_send()

    @pl.when(sp < bands - 1)
    def _():
        down.wait_send()

    @pl.when(sp > 0)
    def _():
        up.wait_send()

    def spread_out(ref, owner):
        for quad in range(groups // 4):
            vecs = [ref[owner, :, pl.ds(LANES * (3 * quad + v), LANES)] for v in range(3)]
            for k, part in enumerate(unpack_four(vecs)):
                blocks[owner, 4 * quad + k] = part
        blocks[owner, groups - 1] = ref[owner, :, pl.ds(LANES * 3 * (groups // 4), LANES)]

    spread_out(result, mem)
    for peer in peers[::-1]:
        back_copy(peer, peer).wait_recv()
        spread_out(returned, peer)

    @pl.loop(0, groups)
    def _(group):
        halves = [swap_blocks([blocks[8 * half + b, group] for b in range(8)]) for half in range(2)]
        for pair in range(4):
            parts = [halves[k % 2][2 * pair + k // 2] for k in range(4)]
            for v, vec in enumerate(pack_four(parts)):
                out_ref[2 * group + pair // 2, :, pl.ds(LANES * (3 * (pair % 2) + v), LANES)] = vec

    for peer in peers:
        back_copy(peer, mem).wait_send()


def cycle(x, diffusivity, coupling, observed, cells, lists, scales, axis_sizes):
    fields, levels = coupling.shape[0], diffusivity.shape[0]
    layers, members, span = x.shape
    tiles = axis_sizes[0]
    everyone = tiles * members
    width = LANES * (-(-layers * TILE_ROWS * TILE_COLS // LANES))
    vmem, smem = pl.BlockSpec(memory_space=pltpu.VMEM), pl.BlockSpec(memory_space=pltpu.SMEM)
    block = pltpu.VMEM((tiles, members, width), F32)
    halo = pltpu.VMEM((layers, members, 3 * LANES), F32)
    semaphores = pltpu.SemaphoreType.DMA((tiles,))
    return pl.pallas_call(
        functools.partial(cycle_kernel, axis_sizes, fields, levels),
        out_shape=jax.ShapeDtypeStruct((layers, members, span), F32),
        in_specs=[pl.BlockSpec(memory_space=pl.ANY), smem, smem, vmem, vmem, vmem, vmem],
        out_specs=vmem,
        scratch_shapes=[
            pltpu.VMEM((layers, members, span), F32),
            halo,
            halo,
            pltpu.VMEM((2, layers, TILE_ROWS, members, LANES), F32),
            pltpu.VMEM((tiles, layers // 2, members, LANES), F32),
            block,
            block,
            block,
            block,
            pltpu.VMEM((COARSE, width), F32),
            pltpu.VMEM((COARSE, width), F32),
            pltpu.VMEM((COARSE, everyone, everyone), F32),
            pltpu.VMEM((COARSE * PANEL, everyone), F32),
            pltpu.SemaphoreType.DMA,
            pltpu.SemaphoreType.DMA((2,)),
            pltpu.SemaphoreType.DMA((2,)),
            semaphores,
            semaphores,
            semaphores,
            semaphores,
        ],
        compiler_params=pltpu.CompilerParams(
            collective_id=0, has_side_effects=True, vmem_limit_bytes=56 * 1024 * 1024
        ),
    )(x, diffusivity, coupling, observed, cells, lists, scales)


def on_device(
    axis_sizes,
    cycle_start_state,
    diffusivity,
    coupling,
    observation_value,
    observation_cell,
    observation_lists,
    localization_weight,
):
    members, fields, levels, span = cycle_start_state.shape
    layers = fields * levels
    y = cycle(
        cycle_start_state.transpose(1, 2, 0, 3).reshape(layers, members, span),
        diffusivity,
        coupling,
        observation_value[0],
        observation_cell[0],
        observation_lists[0, 0],
        localization_weight[0, 0],
        axis_sizes,
    )
    return y.reshape(fields, levels, members, span).transpose(2, 0, 1, 3)


def solution(mesh):
    in_specs = (
        P("mem", None, None, "sp"),
        P(),
        P(),
        P("sp", "mem", None),
        P("sp", "mem", None),
        P("sp", "mem", None, None),
        P("sp", "mem", None, None),
    )
    out_specs = P("mem", None, None, "sp")
    axis_sizes = (mesh.shape["mem"], mesh.shape["sp"])
    return jax.shard_map(
        functools.partial(on_device, axis_sizes), mesh=mesh, in_specs=in_specs, out_specs=out_specs, check_vma=False
    )
```

time: 78.9 us -> 59 us (0.75)
  Pallas kernels: 75.7 us -> 56.9 us
  local copies, waits for them, and re-layouts: 2.64 us -> 1.8 us
    pallas_call x3 -> x1, Pallas kernels: 75.7 us -> 56.9 us  [cycle(): pl.pallas_call(functools.partial(cycle_kernel, axis_sizes, fields, levels...]
    unnamed x15 -> x1, local copies, waits for them, and re-layouts: 2.45 us -> 1.8 us
where the time goes in v1:
time: 59 us; the launch traced here: 58.8 us
  Pallas kernels  56.9 us (96%)
  local copies, waits for them, and re-layouts  1.8 us (3%)
    pallas_call x1, Pallas kernels, cycle(): pl.pallas_call(functools.partial(cycle_kernel, axis_sizes, fields, levels...  56.9 us
    unnamed x1, local copies, waits for them, and re-layouts  1.8 us

profile of v1, /device:TPU:17, one launch (start us, length us, event | category | flops | bytes accessed | tf_op | source)
XLA Modules:
  0.0 58.8 jit_solution(9178433497431792452)
XLA Ops:
  0.0 56.9 %shard_map.73 = f32[18,8,768]{2,1,0:T(8,128)} custom-call(f32[18,8,768]{2,1,0:T(8,128)} %bitcast.11, f32[6]{0:T(128)} %diffusion_ref.1, f32[3,3]{1,0:T(4,128)} %coupling_ref.1, f32[1,512]{1,0:T(1,128)} %bitcast.14, s32[1,512]{1,0:T(1,128)} %bitcast.15, s32[8,256]{1,0:T(8,128)} %bitcast.12, f32[8,256]{1,0:T(8,128)} %bitcast.13), custom_call_target="tpu_custom_call" | custom-call | tf_op jit(solution)/shard_map/pallas_call | solution.py:437
  56.9 1.8 %copy.9 = f32[8,3,6,768]{3,0,2,1:T(8,128)} copy(f32[8,3,6,768]{3,0,2,1:T(8,128)} %bitcast.10) | data formatting | bytes 884736

commit v2 on v1

--- a/solution.py
+++ b/solution.py
@@ -126,9 +126,16 @@
 def swap_blocks(rows):
     rows = list(rows)
     lane = lane_ids(rows[0].shape)
+    edge = [TILE_COLS * k for k in range(9)]
+    between = [(lane >= edge[k]) & (lane < edge[k + 1]) for k in range(8)]
+    keeps = {
+        4: lane < edge[4],
+        2: (lane < edge[2]) | ((lane >= edge[4]) & (lane < edge[6])),
+        1: (between[0] | between[2]) | (between[4] | between[6]),
+    }
     for step in (4, 2, 1):
         width = TILE_COLS * step
-        keep = lane % (2 * width) < width
+        keep = keeps[step]
         for a in range(8):
             if a & step:
                 continue
@@ -278,22 +285,29 @@
         pl.semaphore_signal(barrier, inc=1, device_id={"mem": peer}, device_id_type=MESH)
     pl.semaphore_wait(barrier, tiles - 1 + jnp.minimum(sp, 1) + jnp.minimum(bands - 1 - sp, 1))
 
-    down = pltpu.make_async_remote_copy(
-        src_ref=x_ref.at[:, :, pl.ds(two, two)], dst_ref=north, send_sem=halo_send.at[0], recv_sem=halo_recv.at[0],
-        device_id={"sp": lax.rem(sp + 1, bands)}, device_id_type=MESH,
-    )
-    up = pltpu.make_async_remote_copy(
-        src_ref=x_ref.at[:, :, pl.ds(0, two)], dst_ref=south, send_sem=halo_send.at[1], recv_sem=halo_recv.at[1],
-        device_id={"sp": lax.rem(sp + bands - 1, bands)}, device_id_type=MESH,
-    )
-
-    @pl.when(sp < bands - 1)
-    def _():
-        down.start()
-
-    @pl.when(sp > 0)
-    def _():
-        up.start()
+    def down(level):
+        return pltpu.make_async_remote_copy(
+            src_ref=x_ref.at[:, level, :, pl.ds(two, two)], dst_ref=north.at[:, level],
+            send_sem=halo_send.at[0, level], recv_sem=halo_recv.at[0, level],
+            device_id={"sp": lax.rem(sp + 1, bands)}, device_id_type=MESH,
+        )
+
+    def up(level):
+        return pltpu.make_async_remote_copy(
+            src_ref=x_ref.at[:, level, :, pl.ds(0, two)], dst_ref=south.at[:, level],
+            send_sem=halo_send.at[1, level], recv_sem=halo_recv.at[1, level],
+            device_id={"sp": lax.rem(sp + bands - 1, bands)}, device_id_type=MESH,
+        )
+
+    @pl.loop(0, levels)
+    def _(level):
+        @pl.when(sp < bands - 1)
+        def _():
+            down(level).start()
+
+        @pl.when(sp > 0)
+        def _():
+            up(level).start()
 
     @pl.when(sp == 0)
     def _():
@@ -308,29 +322,28 @@
     total_ref[...] = total
     load.wait()
 
-    @pl.when(sp > 0)
-    def _():
-        down.wait_recv()
-
-    @pl.when(sp < bands - 1)
-    def _():
-        up.wait_recv()
-
     inside_north = jnp.minimum(sp, 1).astype(F32)
     inside_south = jnp.minimum(bands - 1 - sp, 1).astype(F32)
 
     @pl.loop(0, levels)
     def _(level):
+        @pl.when(sp > 0)
+        def _():
+            down(level).wait_recv()
+
+        @pl.when(sp < bands - 1)
+        def _():
+            up(level).wait_recv()
+
         diffusion = diffusion_ref[level]
         own = 1.0 - 4.0 * diffusion
         mix = [[coupling_ref[f, g] + own if f == g else coupling_ref[f, g] for g in range(fields)] for f in range(fields)]
         rows = []
         for f in range(fields):
-            layer = f * levels + level
             line = []
             for ref, starts in ((north, (0,)), (xs, (0, two)), (south, (0,))):
                 for start in starts:
-                    line += row_halves([ref[layer, :, pl.ds(start + LANES * v, LANES)] for v in range(3)])
+                    line += row_halves([ref[f, level, :, pl.ds(start + LANES * v, LANES)] for v in range(3)])
             rows.append(line)
         middle = time_step(rows, diffusion, mix)
         for f in range(fields):
@@ -343,13 +356,14 @@
                 grown[0, layer, r] = final[f][r][0]
                 grown[1, layer, r] = turn(final[f][r][1], 32)
 
-    for half in range(2):
-
-        @pl.loop(0, groups)
-        def _(group):
-            rows = [grown[half, 2 * group + k // 4, k % 4] for k in range(8)]
-            for b, row in enumerate(swap_blocks(rows)):
-                blocks[8 * half + b, group] = row
+    @pl.loop(0, groups // 3)
+    def _(third):
+        for k in range(3):
+            group = 3 * third + k
+            for half in range(2):
+                rows = [grown[half, 2 * group + n // 4, n % 4] for n in range(8)]
+                for b, row in enumerate(swap_blocks(rows)):
+                    blocks[8 * half + b, group] = row
 
     def fill(peer, store):
         for quad in range(groups // 4):
@@ -392,13 +406,15 @@
     for peer in peers:
         block_copy(peer, mem).wait_send()
 
-    @pl.when(sp < bands - 1)
-    def _():
-        down.wait_send()
-
-    @pl.when(sp > 0)
-    def _():
-        up.wait_send()
+    @pl.loop(0, levels)
+    def _(level):
+        @pl.when(sp < bands - 1)
+        def _():
+            down(level).wait_send()
+
+        @pl.when(sp > 0)
+        def _():
+            up(level).wait_send()
 
     def spread_out(ref, owner):
         for quad in range(groups // 4):
@@ -412,13 +428,15 @@
         back_copy(peer, peer).wait_recv()
         spread_out(returned, peer)
 
-    @pl.loop(0, groups)
-    def _(group):
-        halves = [swap_blocks([blocks[8 * half + b, group] for b in range(8)]) for half in range(2)]
-        for pair in range(4):
-            parts = [halves[k % 2][2 * pair + k // 2] for k in range(4)]
-            for v, vec in enumerate(pack_four(parts)):
-                out_ref[2 * group + pair // 2, :, pl.ds(LANES * (3 * (pair % 2) + v), LANES)] = vec
+    @pl.loop(0, groups // 3)
+    def _(third):
+        for k in range(3):
+            group = 3 * third + k
+            halves = [swap_blocks([blocks[8 * half + b, group] for b in range(8)]) for half in range(2)]
+            for pair in range(4):
+                parts = [halves[n % 2][2 * pair + n // 2] for n in range(4)]
+                for v, vec in enumerate(pack_four(parts)):
+                    out_ref[2 * group + pair // 2, :, pl.ds(LANES * (3 * (pair % 2) + v), LANES)] = vec
 
     for peer in peers:
         back_copy(peer, mem).wait_send()
@@ -426,13 +444,14 @@
 
 def cycle(x, diffusivity, coupling, observed, cells, lists, scales, axis_sizes):
     fields, levels = coupling.shape[0], diffusivity.shape[0]
-    layers, members, span = x.shape
+    _, _, members, span = x.shape
+    layers = fields * levels
     tiles = axis_sizes[0]
     everyone = tiles * members
     width = LANES * (-(-layers * TILE_ROWS * TILE_COLS // LANES))
     vmem, smem = pl.BlockSpec(memory_space=pltpu.VMEM), pl.BlockSpec(memory_space=pltpu.SMEM)
     block = pltpu.VMEM((tiles, members, width), F32)
-    halo = pltpu.VMEM((layers, members, 3 * LANES), F32)
+    halo = pltpu.VMEM((fields, levels, members, 3 * LANES), F32)
     semaphores = pltpu.SemaphoreType.DMA((tiles,))
     return pl.pallas_call(
         functools.partial(cycle_kernel, axis_sizes, fields, levels),
@@ -440,7 +459,7 @@
         in_specs=[pl.BlockSpec(memory_space=pl.ANY), smem, smem, vmem, vmem, vmem, vmem],
         out_specs=vmem,
         scratch_shapes=[
-            pltpu.VMEM((layers, members, span), F32),
+            pltpu.VMEM((fields, levels, members, span), F32),
             halo,
             halo,
             pltpu.VMEM((2, layers, TILE_ROWS, members, LANES), F32),
@@ -454,8 +473,8 @@
             pltpu.VMEM((COARSE, everyone, everyone), F32),
             pltpu.VMEM((COARSE * PANEL, everyone), F32),
             pltpu.SemaphoreType.DMA,
-            pltpu.SemaphoreType.DMA((2,)),
-            pltpu.SemaphoreType.DMA((2,)),
+            pltpu.SemaphoreType.DMA((2, levels)),
+            pltpu.SemaphoreType.DMA((2, levels)),
             semaphores,
             semaphores,
             semaphores,
@@ -478,9 +497,8 @@
     localization_weight,
 ):
     members, fields, levels, span = cycle_start_state.shape
-    layers = fields * levels
     y = cycle(
-        cycle_start_state.transpose(1, 2, 0, 3).reshape(layers, members, span),
+        cycle_start_state.transpose(1, 2, 0, 3),
         diffusivity,
         coupling,
         observation_value[0],

time: 59 us -> 56.1 us (0.951)
  Pallas kernels: 56.9 us -> 54.1 us
    pallas_call x1, Pallas kernels: 56.9 us -> 54.1 us  [cycle(): pl.pallas_call(functools.partial(cycle_kernel, axis_sizes, fields, levels...]
where the time goes in v2:
time: 56.1 us; the launch traced here: 55.9 us
  Pallas kernels  54.1 us (96%)
  local copies, waits for them, and re-layouts  1.8 us (3%)
    pallas_call x1, Pallas kernels, cycle(): pl.pallas_call(functools.partial(cycle_kernel, axis_sizes, fields, levels...  54.1 us
    unnamed x1, local copies, waits for them, and re-layouts  1.8 us

profile of v2, /device:TPU:17, one launch (start us, length us, event | category | flops | bytes accessed | tf_op | source)
XLA Modules:
  0.0 55.9 jit_solution(15709955212459889519)
XLA Ops:
  0.0 54.1 %shard_map.73 = f32[18,8,768]{2,1,0:T(8,128)} custom-call(f32[3,6,8,768]{3,2,1,0:T(8,128)} %bitcast.9, f32[6]{0:T(128)} %diffusion_ref.1, f32[3,3]{1,0:T(4,128)} %coupling_ref.1, f32[1,512]{1,0:T(1,128)} %bitcast.12, s32[1,512]{1,0:T(1,128)} %bitcast.13, s32[8,256]{1,0:T(8,128)} %bitcast.10, f32[8,256]{1,0:T(8,128)} %bitcast.11), custom_call_target="tpu_custom_call" | custom-call | tf_op jit(solution)/shard_map/pallas_call | solution.py:456
  54.1 1.8 %copy.9 = f32[8,3,6,768]{3,0,2,1:T(8,128)} copy(f32[8,3,6,768]{3,0,2,1:T(8,128)} %bitcast.8) | data formatting | bytes 884736

commit v3 on v2

--- a/solution.py
+++ b/solution.py
@@ -198,6 +198,13 @@
     return out
 
 
+def regrouped(cells, fields, levels):
+    spots = TILE_ROWS * TILE_COLS
+    layer, spot = lax.div(cells, spots), lax.rem(cells, spots)
+    field, level = lax.div(layer, levels), lax.rem(layer, levels)
+    return (lax.div(level, 2) * fields + field) * (2 * spots) + lax.rem(level, 2) * spots + spot
+
+
 def hat_rows(lanes):
     lane = lax.broadcasted_iota(jnp.int32, (1, lanes), 1) % (TILE_ROWS * TILE_COLS)
     row, col = (lane // TILE_COLS).astype(F32), (lane % TILE_COLS).astype(F32)
@@ -220,10 +227,15 @@
         lead,
         0.0,
     )
-    for c in range(p):
-        s_hi, s_mid, s_lo = split3(dev * weight[c : c + 1, :])
-        g = dot(s_hi, both, NT) + dot(s_mid, both, NT)
-        g_ref[c] = g[:, :members] + g[:, members:] + (dot(s_hi, lo, NT) + dot(s_lo, hi, NT)) + eye
+    stack = 4
+    for c0 in range(0, p, stack):
+        thirds = [split3(dev * weight[c : c + 1, :]) for c in range(c0, c0 + stack)]
+        s_hi, s_mid, s_lo = [jnp.concatenate([third[k] for third in thirds], axis=0) for k in range(3)]
+        g = dot(jnp.concatenate([s_hi, s_mid], axis=0), both, NT)
+        g = g[: stack * members] + g[stack * members :]
+        g = g[:, :members] + g[:, members:] + (dot(s_hi, lo, NT) + dot(s_lo, hi, NT))
+        for k in range(stack):
+            g_ref[c0 + k] = g[members * k : members * (k + 1)] + eye
     gap = total - mean * weight
     g_hi, g_mid, g_lo = split3(gap)
     pull = dot(g_hi, both, NT) + dot(g_mid, both, NT)
@@ -231,23 +243,30 @@
 
     factor_inverses(g_ref, r_ref)
 
-    root = lead**0.5
-    ms = [g_ref[c] for c in range(p)]
-    high = dict(precision=lax.Precision.HIGHEST, preferred_element_type=F32)
-    ys = [lax.dot_general(pull[c : c + 1, :], ms[c], NT, **high) for c in range(p)]
-    ws = [lax.dot_general(ys[c], ms[c], NN, **high) for c in range(p)]
-    hats = hat_rows(lanes)
+    ws = []
+    for c in range(p):
+        m = g_ref[c]
+        y = jnp.sum(m * pull[c : c + 1, :], axis=1, keepdims=True)
+        ws.append(jnp.sum(m * y, axis=0, keepdims=True))
+    return mean, both, hi, ws, hat_rows(lanes)
+
+
+def blend(parts, start, count, g_ref):
+    mean, both, hi, ws, hats = parts
+    root = float(hi.shape[0] - 1) ** 0.5
+    pairs = [split2(g_ref[c, pl.ds(start, count), :] * root + ws[c]) for c in range(COARSE)]
+    high = jnp.concatenate([w_hi for w_hi, _ in pairs], axis=0)
+    low = jnp.concatenate([w_lo for _, w_lo in pairs], axis=0)
+    product = dot(jnp.concatenate([high, high], axis=1), both, NN) + dot(low, hi, NN)
     moved = mean
-    for c in range(p):
-        w_hi, w_lo = split2(ms[c] * root + ws[c])
-        twice = jnp.concatenate([w_hi, w_hi], axis=1)
-        moved = moved + hats[c] * (dot(twice, both, NN) + dot(w_lo, hi, NN))
+    for c in range(COARSE):
+        moved = moved + hats[c] * product[count * c : count * (c + 1)]
     return moved
 
 
 def peer_order(mem):
     side, place, core = mem // 8, mem // 2 % 4, mem % 2
-    far_first = [(1, 2), (0, 2), (1, 1), (1, 3), (1, 0), (0, 1), (0, 3), (0, 0)]
+    far_first = [(1, 2), (1, 1), (1, 3), (1, 0), (0, 2), (0, 1), (0, 3), (0, 0)]
     peers = []
     for d_side, d_place in far_first:
         for d_core in range(2):
@@ -317,16 +336,12 @@
     def _():
         south[...] = jnp.zeros_like(south)
 
-    weight, total = observation_sums(lists_ref[...], scales_ref[...], observed_ref[...], cells_ref[...], width)
-    weight_ref[...] = weight
-    total_ref[...] = total
     load.wait()
 
     inside_north = jnp.minimum(sp, 1).astype(F32)
     inside_south = jnp.minimum(bands - 1 - sp, 1).astype(F32)
 
-    @pl.loop(0, levels)
-    def _(level):
+    def advance(level):
         @pl.when(sp > 0)
         def _():
             down(level).wait_recv()
@@ -356,44 +371,50 @@
                 grown[0, layer, r] = final[f][r][0]
                 grown[1, layer, r] = turn(final[f][r][1], 32)
 
-    @pl.loop(0, groups // 3)
-    def _(third):
-        for k in range(3):
-            group = 3 * third + k
+    def regroup(pair):
+        for f in range(fields):
             for half in range(2):
-                rows = [grown[half, 2 * group + n // 4, n % 4] for n in range(8)]
+                rows = [grown[half, f * levels + 2 * pair + n // 4, n % 4] for n in range(8)]
                 for b, row in enumerate(swap_blocks(rows)):
-                    blocks[8 * half + b, group] = row
-
-    def fill(peer, store):
-        for quad in range(groups // 4):
-            for v, vec in enumerate(pack_four([blocks[peer, 4 * quad + k] for k in range(4)])):
-                store(3 * quad + v, vec)
-        store(3 * (groups // 4), jnp.where(lane_ids((members, LANES)) < HALF, blocks[peer, groups - 1], 0.0))
-
-    def block_copy(peer, slot):
+                    blocks[8 * half + b, fields * pair + f] = row
+
+    def packed_vector(peer, v):
+        lane = lane_ids((members, LANES))
+        quad, j = v // 3, v % 3
+        first = blocks[peer, 4 * quad + j]
+        if 4 * quad + j + 1 == groups:
+            return jnp.where(lane < HALF, first, 0.0)
+        second = turn(blocks[peer, 4 * quad + j + 1], HALF - 32 * j)
+        return jnp.where(lane < HALF - 32 * j, turn(first, -32 * j) if j else first, second)
+
+    def block_copy(part, peer, slot):
+        lanes = pl.ds(LANES * cuts[part], LANES * (cuts[part + 1] - cuts[part]))
         return pltpu.make_async_remote_copy(
-            src_ref=packed.at[peer], dst_ref=landed.at[slot], send_sem=block_send.at[peer], recv_sem=block_recv.at[slot],
+            src_ref=packed.at[peer, :, lanes], dst_ref=landed.at[slot, :, lanes],
+            send_sem=block_send.at[part, peer], recv_sem=block_recv.at[part, slot],
             device_id={"mem": peer}, device_id_type=MESH,
         )
 
-    for peer in peers:
-
-        def store(v, vec):
-            packed[peer, :, pl.ds(LANES * v, LANES)] = vec
-
-        fill(peer, store)
-        block_copy(peer, mem).start()
-
-    def keep(v, vec):
-        landed[mem, :, pl.ds(LANES * v, LANES)] = vec
-
-    fill(mem, keep)
-    for peer in peers[::-1]:
-        block_copy(peer, peer).wait_recv()
-
-    moved = analyse(landed[...].reshape(tiles * members, width), weight_ref[...], total_ref[...], g_ref, r_ref)
-    result[...] = moved.reshape(tiles, members, width)
+    cuts = (0, 4, width // LANES)
+    bounds = (0, 2, levels // 2)
+    for part in range(2):
+        pl.loop(2 * bounds[part], 2 * bounds[part + 1])(advance)
+        pl.loop(bounds[part], bounds[part + 1])(regroup)
+        for peer in peers:
+            for v in range(cuts[part], cuts[part + 1]):
+                packed[peer, :, pl.ds(LANES * v, LANES)] = packed_vector(peer, v)
+            block_copy(part, peer, mem).start()
+        for v in range(cuts[part], cuts[part + 1]):
+            landed[mem, :, pl.ds(LANES * v, LANES)] = packed_vector(mem, v)
+    places = regrouped(cells_ref[...], fields, levels)
+    weight, total = observation_sums(lists_ref[...], scales_ref[...], observed_ref[...], places, width)
+    weight_ref[...] = weight
+    total_ref[...] = total
+    for part in range(2):
+        for peer in peers[::-1]:
+            block_copy(part, peer, peer).wait_recv()
+
+    parts = analyse(landed[...].reshape(tiles * members, width), weight_ref[...], total_ref[...], g_ref, r_ref)
 
     def back_copy(peer, slot):
         return pltpu.make_async_remote_copy(
@@ -401,10 +422,16 @@
             device_id={"mem": peer}, device_id_type=MESH,
         )
 
-    for peer in peers:
-        back_copy(peer, mem).start()
-    for peer in peers:
-        block_copy(peer, mem).wait_send()
+    side = tiles // 2
+    for turn_to in range(2):
+        first = side * ((mem // side + 1 + turn_to) % 2)
+        moved = blend(parts, pl.multiple_of(members * first, members * side), members * side, g_ref)
+        result[pl.ds(first, side)] = moved.reshape(side, members, width)
+        for peer in peers[:side] if turn_to == 0 else peers[side:]:
+            back_copy(peer, mem).start()
+    for part in range(2):
+        for peer in peers:
+            block_copy(part, peer, mem).wait_send()
 
     @pl.loop(0, levels)
     def _(level):
@@ -428,15 +455,16 @@
         back_copy(peer, peer).wait_recv()
         spread_out(returned, peer)
 
-    @pl.loop(0, groups // 3)
-    def _(third):
-        for k in range(3):
-            group = 3 * third + k
+    @pl.loop(0, levels // 2)
+    def _(pair):
+        for f in range(fields):
+            group = fields * pair + f
             halves = [swap_blocks([blocks[8 * half + b, group] for b in range(8)]) for half in range(2)]
-            for pair in range(4):
-                parts = [halves[n % 2][2 * pair + n // 2] for n in range(4)]
+            for two_rows in range(4):
+                parts = [halves[n % 2][2 * two_rows + n // 2] for n in range(4)]
                 for v, vec in enumerate(pack_four(parts)):
-                    out_ref[2 * group + pair // 2, :, pl.ds(LANES * (3 * (pair % 2) + v), LANES)] = vec
+                    layer = f * levels + 2 * pair + two_rows // 2
+                    out_ref[layer, :, pl.ds(LANES * (3 * (two_rows % 2) + v), LANES)] = vec
 
     for peer in peers:
         back_copy(peer, mem).wait_send()
@@ -475,8 +503,8 @@
             pltpu.SemaphoreType.DMA,
             pltpu.SemaphoreType.DMA((2, levels)),
             pltpu.SemaphoreType.DMA((2, levels)),
-            semaphores,
-            semaphores,
+            pltpu.SemaphoreType.DMA((2, tiles)),
+            pltpu.SemaphoreType.DMA((2, tiles)),
             semaphores,
             semaphores,
         ],

time: 56.1 us -> 51.3 us (0.914)
  Pallas kernels: 54.1 us -> 49.2 us
    pallas_call x1, Pallas kernels: 54.1 us -> 49.2 us  [cycle(): pl.pallas_call(functools.partial(cycle_kernel, axis_sizes, fields, levels...]
where the time goes in v3:
time: 51.3 us; the launch traced here: 51 us
  Pallas kernels  49.2 us (96%)
  local copies, waits for them, and re-layouts  1.8 us (4%)
    pallas_call x1, Pallas kernels, cycle(): pl.pallas_call(functools.partial(cycle_kernel, axis_sizes, fields, levels...  49.2 us
    unnamed x1, local copies, waits for them, and re-layouts  1.8 us

profile of v3, /device:TPU:17, one launch (start us, length us, event | category | flops | bytes accessed | tf_op | source)
XLA Modules:
  0.0 51.0 jit_solution(6949391316326501662)
XLA Ops:
  0.0 49.2 %shard_map.73 = f32[18,8,768]{2,1,0:T(8,128)} custom-call(f32[3,6,8,768]{3,2,1,0:T(8,128)} %bitcast.9, f32[6]{0:T(128)} %diffusion_ref.1, f32[3,3]{1,0:T(4,128)} %coupling_ref.1, f32[1,512]{1,0:T(1,128)} %bitcast.12, s32[1,512]{1,0:T(1,128)} %bitcast.13, s32[8,256]{1,0:T(8,128)} %bitcast.10, f32[8,256]{1,0:T(8,128)} %bitcast.11), custom_call_target="tpu_custom_call" | custom-call | tf_op jit(solution)/shard_map/pallas_call | solution.py:484
  49.2 1.8 %copy.9 = f32[8,3,6,768]{3,0,2,1:T(8,128)} copy(f32[8,3,6,768]{3,0,2,1:T(8,128)} %bitcast.8) | data formatting | bytes 884736
